TPU v7x, 32 devices: a whole 2x2x4 slice. The times are simulated.
32 devices in a mesh: shots: 2 (over x), gx: 16 (over z, y, core).
Axes of the slice: x: 2, y: 2, z: 4, core: 2. Of those that a mesh axis runs over, the one named last changes fastest.
Arguments:
- velocity: float32 [256, 24, 128], P('gx'), may hold values from 0.05 to 0.18
- source_prior: float32 [512, 24, 128], P(('shots', 'gx')), parts along dimension 0, may hold values from -6 to 6
- source_now: float32 [512, 24, 128], P(('shots', 'gx')), parts along dimension 0, may hold values from -6 to 6
- record_prior: float32 [512, 24, 128], P(('shots', 'gx')), parts along dimension 0, may hold values from -6 to 6
- record_now: float32 [512, 24, 128], P(('shots', 'gx')), parts along dimension 0, may hold values from -6 to 6
- source_inline: int32 [32], P('shots'), parts along dimension 0, may hold values from 0 to 255
- source_crossline: int32 [32], P('shots'), parts along dimension 0, may hold values from 0 to 23
- source_pulse: float32 [32, 2], P('shots'), parts along dimension 0, may hold values from -12 to 12
- receiver_inline: int32 [2048], P('shots'), parts along dimension 0, may hold values from 0 to 255
- receiver_crossline: int32 [2048], P('shots'), parts along dimension 0, may hold values from 0 to 23
- receiver_trace: float32 [2048, 2], P('shots'), parts along dimension 0, may hold values from -12 to 12
- offsets: int32 [17], replicated, may hold values from -8 to 8
Outputs:
- images: bfloat16 [34, 256, 24, 128], P('shots', 'gx'), parts along dimension 0
- adjoint_source: float32 [512, 24, 128], P(('shots', 'gx')), parts along dimension 0
- adjoint_receiver: float32 [512, 24, 128], P(('shots', 'gx')), parts along dimension 0
There are 2 independent parts, one for each index of `shots`. A program takes and returns all parts, laid end to end along the dimension named above; an argument that names none is the same for every part. Nothing has to cross between parts.
All inputs are finite; a program needn't handle non-finite values.
Results may differ from a plain program's by a relative error of at most 0.001.
Values sent between devices are 32-bit elements; how exact they have to be, the bound alone decides.
A program may use at most 128 MiB of HBM per device.

v0:
```python
import jax
import jax.numpy as jnp
from jax import lax
from jax.sharding import PartitionSpec as P

STEPS = 2
NLAG = 17
LAG_MAX = 8


stencil = (-205.0 / 72.0, 8.0 / 5.0, -1.0 / 5.0, 8.0 / 315.0, -1.0 / 560.0)
source_depth = 3
record_depth = 1


def extended(shard, sides, width):
    for axis, dim in sides:
        count, length = (lax.axis_size(axis), shard.shape[dim])
        up = [(i, (i + 1) % count) for i in range(count - 1)]
        down = [(j, i) for i, j in up]
        last = lax.slice_in_dim(shard, length - width, length, axis=dim)
        first = lax.slice_in_dim(shard, 0, width, axis=dim)
        before = lax.ppermute(last, axis, up)
        after = lax.ppermute(first, axis, down)
        shard = jnp.concatenate([before, shard, after], axis=dim)
    return shard


def from_behind(block, axis, distance):
    devices = range(lax.axis_size(axis))
    route = [(i - distance, i) for i in devices if i - distance in devices]
    return lax.ppermute(block, axis, route)


def laplace_trim(wide):
    length = wide.shape[1] - 8
    cells_y = wide.shape[2]
    cells_z = wide.shape[3]
    padded = jnp.pad(wide, ((0, 0), (0, 0), (4, 4), (4, 4)))
    summed = 3.0 * stencil[0] * padded[:, 4 : 4 + length, 4 : 4 + cells_y, 4 : 4 + cells_z]
    for offset in range(1, 5):
        beside_all = padded[:, 4 + offset : 4 + offset + length, 4 : 4 + cells_y, 4 : 4 + cells_z]
        beside_all = (
            beside_all
            + padded[:, 4 - offset : 4 - offset + length, 4 : 4 + cells_y, 4 : 4 + cells_z]
        )
        beside_all = (
            beside_all
            + padded[:, 4 : 4 + length, 4 + offset : 4 + offset + cells_y, 4 : 4 + cells_z]
        )
        beside_all = (
            beside_all
            + padded[:, 4 : 4 + length, 4 - offset : 4 - offset + cells_y, 4 : 4 + cells_z]
        )
        beside_all = (
            beside_all
            + padded[:, 4 : 4 + length, 4 : 4 + cells_y, 4 + offset : 4 + offset + cells_z]
        )
        beside_all = (
            beside_all
            + padded[:, 4 : 4 + length, 4 : 4 + cells_y, 4 - offset : 4 - offset + cells_z]
        )
        summed = summed + stencil[offset] * beside_all
    return summed


def injection(place_x, place_y, amplitude, anchor, count_x, count_y):
    hits_x = (place_x[:, None] - anchor == jnp.arange(count_x, dtype=jnp.int32)[None, :]).astype(
        jnp.float32
    ) * amplitude[:, None]
    hits_y = (place_y[:, None] == jnp.arange(count_y, dtype=jnp.int32)[None, :]).astype(jnp.float32)
    return jnp.einsum("sx,sy->xy", hits_x, hits_y, precision=lax.Precision.HIGHEST)


def accumulate_terms(squares, offsets, length):
    weights = (offsets * offsets).astype(jnp.float32) / (LAG_MAX * LAG_MAX * NLAG)

    def accumulate(index, carry):
        shift_cells = offsets[index]
        from_record = lax.dynamic_slice_in_dim(squares[1], 2 * LAG_MAX + 2 * shift_cells, length, 0)
        from_source = lax.dynamic_slice_in_dim(squares[0], 2 * LAG_MAX - 2 * shift_cells, length, 0)
        return carry + weights[index] * jnp.stack([from_record, from_source])

    empty = jnp.zeros((2, length) + squares.shape[2:], jnp.float32)
    return lax.fori_loop(0, NLAG, accumulate, empty)


def image_stack(wide, reach, offsets, extent):

    def single(shift_cells):
        left = lax.dynamic_slice_in_dim(wide[0], reach - shift_cells, extent, 0)
        right = lax.dynamic_slice_in_dim(wide[1], reach + shift_cells, extent, 0)
        return (left * right).astype(jnp.bfloat16)

    return jax.vmap(single)(offsets)


def per_device(
    velocity,
    source_prior,
    source_now,
    record_prior,
    record_now,
    source_inline,
    source_crossline,
    source_pulse,
    receiver_inline,
    receiver_crossline,
    receiver_trace,
    offsets,
):
    extent = velocity.shape[0]
    cells_y = velocity.shape[1]
    anchor = lax.axis_index("gx") * extent
    current = jnp.stack([source_now, record_now])
    previous = jnp.stack([source_prior, record_prior])
    for moment in range(STEPS):
        wide = extended(current, (("gx", 1),), 4)
        upcoming = 2.0 * current - previous + velocity[None] * laplace_trim(wide)
        field = upcoming
        source_plane = injection(
            source_inline, source_crossline, source_pulse[:, moment], anchor, extent, cells_y
        )
        record_plane = injection(
            receiver_inline, receiver_crossline, receiver_trace[:, moment], anchor, extent, cells_y
        )
        field = field.at[0, :, :, source_depth].add(source_plane)
        upcoming = field.at[1, :, :, record_depth].add(record_plane)
        previous, current = (current, upcoming)
    wide = extended(current, (("gx", 1),), LAG_MAX)
    images = image_stack(wide, LAG_MAX, offsets, extent)
    squares = jnp.pad(current * current, ((0, 0), (4 * LAG_MAX, 4 * LAG_MAX), (0, 0), (0, 0)))
    terms = accumulate_terms(squares, offsets, extent + 4 * LAG_MAX)
    lower_rim = terms[:, : 2 * LAG_MAX]
    upper_rim = terms[:, extent + 2 * LAG_MAX :]
    middle = terms[:, 2 * LAG_MAX : 2 * LAG_MAX + extent]
    from_lower = from_behind(upper_rim, "gx", 1)
    from_upper = from_behind(lower_rim, "gx", -1)
    middle = middle.at[:, : 2 * LAG_MAX].add(from_lower)
    middle = middle.at[:, extent - 2 * LAG_MAX :].add(from_upper)
    return (images, current[0] * middle[0], current[1] * middle[1])


def solution(mesh):
    in_specs = (
        P("gx", None, None),
        P(("shots", "gx"), None, None),
        P(("shots", "gx"), None, None),
        P(("shots", "gx"), None, None),
        P(("shots", "gx"), None, None),
        P("shots"),
        P("shots"),
        P("shots", None),
        P("shots"),
        P("shots"),
        P("shots", None),
        P(),
    )
    out_specs = (
        P("shots", "gx", None, None),
        P(("shots", "gx"), None, None),
        P(("shots", "gx"), None, None),
    )
    return jax.shard_map(
        per_device, mesh=mesh, in_specs=in_specs, out_specs=out_specs, check_vma=False
    )
```

profile of v0, /device:TPU:8, one launch (start us, length us, event | category | flops | bytes accessed | tf_op | source)
XLA Modules:
  0.0 124.2 jit_solution(5781560303846381513)
XLA Ops:
  0.7 1.0 fusion.59
  1.6 1.9 %collective-permute-start.1 = (f32[2,4,24,128]{3,2,1,0:T(8,128)S(1)}, f32[2,4,24,128]{3,2,1,0:T(8,128)S(1)}, u32[]{:S(2)}, u32[]{:S(2)}) collective-permute-start(f32[2,4,24,128]{3,2,1,0:T(8,128)S(1)} %get-tuple-element.308), channel_id=1, source_target_pairs={{0,1},{1,2},{2,3},{3,4},{4,5},{5,6},{6,7},{7,8},{8,9},{9,10},{10,1... | collective-permute-start | bytes 294920 | tf_op jit(solution)/shard_map/ppermute | solution.py:23
  3.6 4.5 %collective-permute-start = (f32[2,4,24,128]{3,2,1,0:T(8,128)S(1)}, f32[2,4,24,128]{3,2,1,0:T(8,128)S(1)}, u32[]{:S(2)}, u32[]{:S(2)}) collective-permute-start(f32[2,4,24,128]{3,2,1,0:T(8,128)S(1)} %get-tuple-element.309), channel_id=1, source_target_pairs={{1,0},{2,1},{3,2},{4,3},{5,4},{6,5},{7,6},{8,7},{9,8},{10,9},{11,1... | collective-permute-start | bytes 294920 | tf_op jit(solution)/shard_map/ppermute | solution.py:24
  8.1 1.2 convert_multiply_fusion
  12.7 0.8 fusion.82
  13.5 1.7 %convolution_bitcast_fusion.2 = f32[1,16,24,1]{2,1,3,0:T(8,128)S(1)} fusion(s32[1024]{0:T(1024)} %param.39, f32[1024]{0:T(1024)S(1)} %bitcast.56, s32[1024]{0:T(1024)S(1)} %broadcast_subtract_fusion), kind=kOutput, calls=%fused_computation.21 | convolution fusion | flops 4775936 | bytes 13824 | tf_op jit(solution)/shard_map/sx,sy->xy/dot_general | solution.py:72
  15.2 1.7 %convolution_bitcast_fusion = f32[1,16,24,1]{2,1,3,0:T(8,128)S(1)} fusion(f32[1024]{0:T(1024)S(1)} %bitcast.55, s32[1024]{0:T(1024)} %param.39, s32[1024]{0:T(1024)S(1)} %broadcast_subtract_fusion), kind=kOutput, calls=%fused_computation.19 | convolution fusion | flops 4775936 | bytes 13824 | tf_op jit(solution)/shard_map/sx,sy->xy/dot_general | solution.py:72
  17.7 2.0 %and_reduce_fusion = pred[]{:T(512)} fusion(s32[4]{0:T(128)S(1)} %copy-done.5, s32[1]{0:T(128)} %get-tuple-element.316, s32[1]{0:T(128)} %constant.273.clone.1, s32[1]{0:T(128)} %get-tuple-element.317), kind=kLoop, calls=%fused_computation.152 | loop fusion | flops 27 | bytes 29 | tf_op jit(solution)/shard_map/reduce.6
  20.8 1.6 %fusion.41 = f32[2,16,24,128]{3,2,1,0:T(8,128)S(1)} fusion(f32[2,24,32,136]{3,2,1,0:T(8,128)S(1)} %select_maximum_fusion.2, f32[2,20,24,128]{3,2,1,0:T(8,128)S(1)} %get-tuple-element.307, f32[2,20,24,128]{3,2,1,0:T(8,128)S(1)} %get-tuple-element.306, f32[1,16,24,128]{3,2,1,0:T(8,128)S(1)} %bitcast.53, f32[1,16,24,128]{3,2,1,0:T(8,128)S(1)} %bitcast.54, ...), kind=kLoop, calls=%fused_computation.91 | loop fusion | flops 3440640 | bytes 10813440 | tf_op jit(solution)/shard_map/add | solution.py:119
  22.4 2.1 %add_select_fusion.1 = f32[1,16,24,1]{3,2,1,0:T(8,128)S(1)} fusion(f32[1,16,24,1]{3,2,1,0:T(8,128)S(1)} %copy.90, f32[2,16,24,128]{3,2,1,0:T(8,128)S(1)} %fusion.41, s32[]{:T(128)} %bitcast.4, s32[]{:T(128)} %bitcast.5, pred[]{:T(512)} %and_reduce_fusion), kind=kLoop, calls=%fused_computation.120 | loop fusion | flops 768 | bytes 4617 | tf_op jit(solution)/shard_map/select.6
  24.5 2.6 %scatter-add.14 = f32[2,16,24,128]{3,2,1,0:T(8,128)S(1)} dynamic-update-slice(f32[2,16,24,128]{3,2,1,0:T(8,128)S(1)} %fusion.41, f32[1,16,24,1]{3,2,1,0:T(8,128)S(1)} %add_select_fusion.1, s32[]{:T(128)} %bitcast.4, s32[]{:T(128)} %constant.271.clone.1, s32[]{:T(128)} %constant.271.clone.1, s32[]{:T(128)} %bitcast.5) | dynamic-update-slice | bytes 3076 | tf_op jit(solution)/shard_map/scatter-add | solution.py:127
  27.2 1.3 %scatter-add.15 = f32[2,16,24,128]{3,2,1,0:T(8,128)S(1)} dynamic-update-slice(f32[2,16,24,128]{3,2,1,0:T(8,128)S(1)} %scatter-add.14, f32[1,16,24,1]{3,2,1,0:T(8,128)S(1)} %slice_add_fusion.25, s32[]{:T(128)} %constant.278.clone.1, s32[]{:T(128)} %constant.271.clone.1, s32[]{:T(128)} %constant.271.clone.1, s32[]{:T(128)} %constant.278.clone.1) | dynamic-update-slice | bytes 3076 | tf_op jit(solution)/shard_map/scatter-add | solution.py:128
  28.5 1.9 %collective-permute-start.2 = (f32[2,4,24,128]{3,2,1,0:T(8,128)S(1)}, f32[2,4,24,128]{3,2,1,0:T(8,128)S(1)}, u32[]{:S(2)}, u32[]{:S(2)}) collective-permute-start(f32[2,4,24,128]{3,2,1,0:T(8,128)S(1)} %get-tuple-element.304), channel_id=1, source_target_pairs={{1,0},{2,1},{3,2},{4,3},{5,4},{6,5},{7,6},{8,7},{9,8},{10,9},{11,1... | collective-permute-start | bytes 294920 | tf_op jit(solution)/shard_map/ppermute | solution.py:24
  30.5 2.4 %collective-permute-start.3 = (f32[2,4,24,128]{3,2,1,0:T(8,128)S(1)}, f32[2,4,24,128]{3,2,1,0:T(8,128)S(1)}, u32[]{:S(2)}, u32[]{:S(2)}) collective-permute-start(f32[2,4,24,128]{3,2,1,0:T(8,128)S(1)} %get-tuple-element.305), channel_id=1, source_target_pairs={{0,1},{1,2},{2,3},{3,4},{4,5},{5,6},{6,7},{7,8},{8,9},{9,10},{10,1... | collective-permute-start | bytes 294920 | tf_op jit(solution)/shard_map/ppermute | solution.py:23
  33.3 4.0 %collective-permute-done.3 = f32[2,4,24,128]{3,2,1,0:T(8,128)S(1)} collective-permute-done((f32[2,4,24,128]{3,2,1,0:T(8,128)S(1)}, f32[2,4,24,128]{3,2,1,0:T(8,128)S(1)}, u32[]{:S(2)}, u32[]{:S(2)}) %collective-permute-start.3) | collective-permute-done | bytes 98336 | tf_op jit(solution)/shard_map/ppermute | solution.py:23
  37.8 1.6 %fusion.16 = f32[2,16,24,128]{3,2,1,0:T(8,128)S(1)} fusion(f32[2,16,24,128]{3,2,1,0:T(8,128)S(1)} %scatter-add.15, f32[2,4,24,128]{3,2,1,0:T(8,128)S(1)} %collective-permute-done.3, f32[2,4,24,128]{3,2,1,0:T(8,128)S(1)} %collective-permute-done.2, f32[2,24,32,136]{3,2,1,0:T(8,128)S(1)} %select_maximum_fusion, f32[1,16,24,128]{3,2,1,0:T(8,128)S(1)} %bitcast.52, ...), kind=kLoop, calls=%fused_computation.57 | loop fusion | flops 4128768 | bytes 7864320 | tf_op jit(solution)/shard_map/add | solution.py:119
  39.4 2.1 %add_select_fusion = f32[1,16,24,1]{3,2,1,0:T(8,128)S(1)} fusion(f32[1,16,24,1]{3,2,1,0:T(8,128)S(1)} %copy.92, f32[2,16,24,128]{3,2,1,0:T(8,128)S(1)} %fusion.16, s32[]{:T(128)} %bitcast.4, s32[]{:T(128)} %bitcast.5, pred[]{:T(512)} %and_reduce_fusion), kind=kLoop, calls=%fused_computation.119 | loop fusion | flops 768 | bytes 4617 | tf_op jit(solution)/shard_map/select.8
  41.5 2.6 %scatter-add.16 = f32[2,16,24,128]{3,2,1,0:T(8,128)S(1)} dynamic-update-slice(f32[2,16,24,128]{3,2,1,0:T(8,128)S(1)} %fusion.16, f32[1,16,24,1]{3,2,1,0:T(8,128)S(1)} %add_select_fusion, s32[]{:T(128)} %bitcast.4, s32[]{:T(128)} %constant.271.clone.1, s32[]{:T(128)} %constant.271.clone.1, s32[]{:T(128)} %bitcast.5) | dynamic-update-slice | bytes 3076 | tf_op jit(solution)/shard_map/scatter-add | solution.py:127
  44.2 1.3 %scatter-add.19 = f32[2,16,24,128]{3,2,1,0:T(8,128)S(1)} dynamic-update-slice(f32[2,16,24,128]{3,2,1,0:T(8,128)S(1)} %scatter-add.16, f32[1,16,24,1]{3,2,1,0:T(8,128)S(1)} %slice_add_fusion.24, s32[]{:T(128)} %constant.278.clone.1, s32[]{:T(128)} %constant.271.clone.1, s32[]{:T(128)} %constant.271.clone.1, s32[]{:T(128)} %constant.278.clone.1) | dynamic-update-slice | bytes 3076 | tf_op jit(solution)/shard_map/scatter-add | solution.py:128
  45.6 0.8 fusion.80
  46.4 1.9 %collective-permute-start.4 = (f32[2,8,24,128]{3,2,1,0:T(8,128)}, f32[2,8,24,128]{3,2,1,0:T(8,128)}, u32[]{:S(2)}, u32[]{:S(2)}) collective-permute-start(f32[2,8,24,128]{3,2,1,0:T(8,128)} %get-tuple-element.302), channel_id=1, source_target_pairs={{0,1},{1,2},{2,3},{3,4},{4,5},{5,6},{6,7},{7,8},{8,9},{9,10},{10,1... | collective-permute-start | bytes 589832 | tf_op jit(solution)/shard_map/ppermute | solution.py:23
  48.3 4.5 %collective-permute-start.5 = (f32[2,8,24,128]{3,2,1,0:T(8,128)}, f32[2,8,24,128]{3,2,1,0:T(8,128)}, u32[]{:S(2)}, u32[]{:S(2)}) collective-permute-start(f32[2,8,24,128]{3,2,1,0:T(8,128)} %get-tuple-element.303), channel_id=1, source_target_pairs={{1,0},{2,1},{3,2},{4,3},{5,4},{6,5},{7,6},{8,7},{9,8},{10,9},{11,1... | collective-permute-start | bytes 589832 | tf_op jit(solution)/shard_map/ppermute | solution.py:24
  53.0 52.0 %while.25 = (s32[]{:T(128)}, f32[2,48,24,128]{3,2,1,0:T(8,128)S(1)}, f32[17]{0:T(128)S(1)}, f32[2,80,24,128]{3,2,1,0:T(8,128)S(1)}, s32[17]{0:T(128)S(1)}, /*ind...) while((s32[]{:T(128)}, f32[2,48,24,128]{3,2,1,0:T(8,128)S(1)}, ...), condition=%wide.region_2.3_spmd.clone, body=%wide.region_1.2_spmd.clone.sunk | while | flops 1179660 | bytes 9830659 | solution.py:85
  55.1 0.9 fusion.87
  58.1 0.9 fusion.87
  61.2 0.9 fusion.87
  64.3 0.9 fusion.87
  67.3 0.9 fusion.87
  70.4 0.9 fusion.87
  73.5 0.9 fusion.87
  76.5 0.9 fusion.87
  79.6 0.9 fusion.87
  82.6 0.9 fusion.87
  85.7 0.9 fusion.87
  88.8 0.9 fusion.87
  91.8 0.9 fusion.87
  94.9 0.9 fusion.87
  97.9 0.9 fusion.87
  101.0 0.9 fusion.87
  104.0 0.9 fusion.87
  105.0 0.8 fusion.79
  105.8 1.9 %collective-permute-start.6 = (f32[2,16,24,128]{3,2,1,0:T(8,128)}, f32[2,16,24,128]{3,2,1,0:T(8,128)S(1)}, u32[]{:S(2)}, u32[]{:S(2)}) collective-permute-start(f32[2,16,24,128]{3,2,1,0:T(8,128)} %get-tuple-element.296), channel_id=1, source_target_pairs={{0,1},{1,2},{2,3},{3,4},{4,5},{5,6},{6,7},{7,8},{8,9},{9,10},{10,1... | collective-permute-start | bytes 1179656 | tf_op jit(solution)/shard_map/ppermute | solution.py:32
  107.7 4.5 %collective-permute-start.7 = (f32[2,16,24,128]{3,2,1,0:T(8,128)S(1)}, f32[2,16,24,128]{3,2,1,0:T(8,128)S(1)}, u32[]{:S(2)}, u32[]{:S(2)}) collective-permute-start(f32[2,16,24,128]{3,2,1,0:T(8,128)S(1)} %get-tuple-element.297), channel_id=1, source_target_pairs={{1,0},{2,1},{3,2},{4,3},{5,4},{6,5},{7,6},{8,7},{9,8},{10,9},{11,1... | collective-permute-start | bytes 1179656 | tf_op jit(solution)/shard_map/ppermute | solution.py:32
  112.3 1.1 pad_maximum_fusion
  113.5 2.7 %gather_fusion.1 = f32[17,16,24,128]{3,2,1,0:T(8,128)} fusion(f32[32,24,128]{2,1,0:T(8,128)S(1)} %get-tuple-element.300, s32[17]{0:T(128)S(1)} %get-tuple-element.314), kind=kCustom, calls=%fused_computation.1 | custom fusion | bytes 6684876 | tf_op jit(solution)/shard_map/vmap()/gather | solution.py:92
  116.1 2.7 %gather_fusion = f32[17,16,24,128]{3,2,1,0:T(8,128)} fusion(f32[32,24,128]{2,1,0:T(8,128)S(1)} %get-tuple-element.301, s32[17]{0:T(128)S(1)} %get-tuple-element.315), kind=kCustom, calls=%fused_computation | custom fusion | bytes 6684876 | tf_op jit(solution)/shard_map/vmap()/gather | solution.py:91
  118.8 4.5 %multiply_convert_fusion = bf16[17,16,24,128]{3,2,1,0:T(8,128)(2,1)} fusion(f32[17,16,24,128]{3,2,1,0:T(8,128)} %gather_fusion, f32[17,16,24,128]{3,2,1,0:T(8,128)} %gather_fusion.1), kind=kLoop, calls=%fused_computation.6 | loop fusion | flops 1671168 | bytes 8355840 | tf_op jit(solution)/shard_map/vmap()/convert_element_type | solution.py:93
  123.4 0.8 fusion.56
  (120 shorter events, 30.7 us)
Async XLA Ops:
  0.6 17.1 %copy-start.5 = (s32[4]{0:T(128)S(1)}, s32[4]{0:T(128)}, u32[]{:S(2)}) copy-start(s32[4]{0:T(128)} %constant.274.clone.1) | copy-start | bytes 52
  0.6 19.1 %copy-start.1 = (f32[16,24,128]{2,1,0:T(8,128)S(1)}, f32[16,24,128]{2,1,0:T(8,128)}, u32[]{:S(2)}) copy-start(f32[16,24,128]{2,1,0:T(8,128)} %param.34) | copy-start | bytes 589828
  0.7 19.1 %copy-start = (f32[16,24,128]{2,1,0:T(8,128)S(1)}, f32[16,24,128]{2,1,0:T(8,128)}, u32[]{:S(2)}) copy-start(f32[16,24,128]{2,1,0:T(8,128)} %param.32) | copy-start | bytes 589828
  0.7 16.6 %copy-start.6 = (s32[16]{0:T(128)S(1)}, s32[16]{0:T(128)}, u32[]{:S(2)}) copy-start(s32[16]{0:T(128)} %param.36) | copy-start | bytes 196
  1.6 18.1 %collective-permute-start.1 = (f32[2,4,24,128]{3,2,1,0:T(8,128)S(1)}, f32[2,4,24,128]{3,2,1,0:T(8,128)S(1)}, u32[]{:S(2)}, u32[]{:S(2)}) collective-permute-start(f32[2,4,24,128]{3,2,1,0:T(8,128)S(1)} %get-tuple-element.308), channel_id=1, source_target_pairs={{0,1},{1,2},{2,3},{3,4},{4,5},{5,6},{6,7},{7,8},{8,9},{9,10},{10,1... | collective-permute-start | bytes 294920 | tf_op jit(solution)/shard_map/ppermute | solution.py:23
  3.6 16.2 %collective-permute-start = (f32[2,4,24,128]{3,2,1,0:T(8,128)S(1)}, f32[2,4,24,128]{3,2,1,0:T(8,128)S(1)}, u32[]{:S(2)}, u32[]{:S(2)}) collective-permute-start(f32[2,4,24,128]{3,2,1,0:T(8,128)S(1)} %get-tuple-element.309), channel_id=1, source_target_pairs={{1,0},{2,1},{3,2},{4,3},{5,4},{6,5},{7,6},{8,7},{9,8},{10,9},{11,1... | collective-permute-start | bytes 294920 | tf_op jit(solution)/shard_map/ppermute | solution.py:24
  12.0 5.3 %copy-start.9 = (s32[16]{0:T(128)}, s32[16]{0:T(128)S(1)}, u32[]{:S(2)}) copy-start(s32[16]{0:T(128)S(1)} %broadcast_subtract_fusion.1) | copy-start | bytes 196
  19.7 0.9 copy-start.2
  19.7 1.0 copy-start.3
  19.7 1.1 copy-start.4
  22.4 10.5 %copy-start.10 = (s32[16]{0:T(128)S(1)}, s32[16]{0:T(128)}, u32[]{:S(2)}) copy-start(s32[16]{0:T(128)} %copy-done.9) | copy-start | bytes 196
  28.5 4.8 %collective-permute-start.2 = (f32[2,4,24,128]{3,2,1,0:T(8,128)S(1)}, f32[2,4,24,128]{3,2,1,0:T(8,128)S(1)}, u32[]{:S(2)}, u32[]{:S(2)}) collective-permute-start(f32[2,4,24,128]{3,2,1,0:T(8,128)S(1)} %get-tuple-element.304), channel_id=1, source_target_pairs={{1,0},{2,1},{3,2},{4,3},{5,4},{6,5},{7,6},{8,7},{9,8},{10,9},{11,1... | collective-permute-start | bytes 294920 | tf_op jit(solution)/shard_map/ppermute | solution.py:24
  30.5 6.8 %collective-permute-start.3 = (f32[2,4,24,128]{3,2,1,0:T(8,128)S(1)}, f32[2,4,24,128]{3,2,1,0:T(8,128)S(1)}, u32[]{:S(2)}, u32[]{:S(2)}) collective-permute-start(f32[2,4,24,128]{3,2,1,0:T(8,128)S(1)} %get-tuple-element.305), channel_id=1, source_target_pairs={{0,1},{1,2},{2,3},{3,4},{4,5},{5,6},{6,7},{7,8},{8,9},{9,10},{10,1... | collective-permute-start | bytes 294920 | tf_op jit(solution)/shard_map/ppermute | solution.py:23
  45.6 7.4 %copy-start.7 = (s32[17]{0:T(128)S(1)}, s32[17]{0:T(128)}, u32[]{:S(2)}) copy-start(s32[17]{0:T(128)} %param.41) | copy-start | bytes 208
  45.6 7.4 %copy-start.8 = (f32[17]{0:T(128)S(1)}, f32[17]{0:T(128)}, u32[]{:S(2)}) copy-start(f32[17]{0:T(128)} %convert_multiply_fusion) | copy-start | bytes 208
  46.4 65.9 %collective-permute-start.4 = (f32[2,8,24,128]{3,2,1,0:T(8,128)}, f32[2,8,24,128]{3,2,1,0:T(8,128)}, u32[]{:S(2)}, u32[]{:S(2)}) collective-permute-start(f32[2,8,24,128]{3,2,1,0:T(8,128)} %get-tuple-element.302), channel_id=1, source_target_pairs={{0,1},{1,2},{2,3},{3,4},{4,5},{5,6},{6,7},{7,8},{8,9},{9,10},{10,1... | collective-permute-start | bytes 589832 | tf_op jit(solution)/shard_map/ppermute | solution.py:23
  48.3 64.0 %collective-permute-start.5 = (f32[2,8,24,128]{3,2,1,0:T(8,128)}, f32[2,8,24,128]{3,2,1,0:T(8,128)}, u32[]{:S(2)}, u32[]{:S(2)}) collective-permute-start(f32[2,8,24,128]{3,2,1,0:T(8,128)} %get-tuple-element.303), channel_id=1, source_target_pairs={{1,0},{2,1},{3,2},{4,3},{5,4},{6,5},{7,6},{8,7},{9,8},{10,9},{11,1... | collective-permute-start | bytes 589832 | tf_op jit(solution)/shard_map/ppermute | solution.py:24
  105.8 17.5 %collective-permute-start.6 = (f32[2,16,24,128]{3,2,1,0:T(8,128)}, f32[2,16,24,128]{3,2,1,0:T(8,128)S(1)}, u32[]{:S(2)}, u32[]{:S(2)}) collective-permute-start(f32[2,16,24,128]{3,2,1,0:T(8,128)} %get-tuple-element.296), channel_id=1, source_target_pairs={{0,1},{1,2},{2,3},{3,4},{4,5},{5,6},{6,7},{7,8},{8,9},{9,10},{10,1... | collective-permute-start | bytes 1179656 | tf_op jit(solution)/shard_map/ppermute | solution.py:32
  107.7 15.6 %collective-permute-start.7 = (f32[2,16,24,128]{3,2,1,0:T(8,128)S(1)}, f32[2,16,24,128]{3,2,1,0:T(8,128)S(1)}, u32[]{:S(2)}, u32[]{:S(2)}) collective-permute-start(f32[2,16,24,128]{3,2,1,0:T(8,128)S(1)} %get-tuple-element.297), channel_id=1, source_target_pairs={{1,0},{2,1},{3,2},{4,3},{5,4},{6,5},{7,6},{8,7},{9,8},{10,9},{11,1... | collective-permute-start | bytes 1179656 | tf_op jit(solution)/shard_map/ppermute | solution.py:32
where the time goes:
time: 125 us; the launch traced here: 124 us
  local copies, waits for them, and re-layouts  42.3 us (34%)
  other arithmetic  37.4 us (30%)
  starting transfers between devices  23.7 us (19%)
  loops' own time  11.9 us (10%)
  waiting for transfers between devices  3.98 us (3%)
  matrix products  3.93 us (3%)
    add x17, other arithmetic, accumulate(): return carry + weights[index] * jnp.stack([from_record, from_source])  16.1 us
    another operation x1, loops' own time, accumulate_terms(): return lax.fori_loop(0, NLAG, accumulate, empty)  11.9 us
    ppermute x3, starting transfers between devices, extended(): after = lax.ppermute(first, axis, down)  11 us
    dynamic_slice x17, local copies, waits for them, and re-layouts, accumulate(): return carry + weights[index] * jnp.stack([from_record, from_source])  10.4 us
    dynamic_slice x17, local copies, waits for them, and re-layouts, accumulate(): shift_cells = offsets[index]  9.9 us
    ppermute x2, starting transfers between devices, from_behind(): return lax.ppermute(block, axis, route)  6.45 us
    ppermute x3, starting transfers between devices, extended(): before = lax.ppermute(last, axis, up)  6.24 us
    another operation x4, other arithmetic  6.12 us
  transfers between devices with their start and end apart: 8, of which 1 were waited for; matrix products, arithmetic and copies ran while one was open for 52% of the time, Pallas kernels for 0%

commit v1 on v0

v1 whole, which is shorter than its diff:
```python
import functools

import jax
import jax.numpy as jnp
from jax import lax
from jax.experimental import pallas as pl
from jax.experimental.pallas import tpu as pltpu
from jax.sharding import PartitionSpec as P

STEPS = 2
LAG_MAX = 8
REACH = 2 * LAG_MAX
RIM = 4

stencil = (-205.0 / 72.0, 8.0 / 5.0, -1.0 / 5.0, 8.0 / 315.0, -1.0 / 560.0)
depths = (3, 1)
LEFT_PAD = 8


def split_halves(x):
    high = x.astype(jnp.bfloat16)
    low = (x - high.astype(jnp.float32)).astype(jnp.bfloat16)
    return high, low


def depth_band(cells_z):
    rows = lax.broadcasted_iota(jnp.int32, (cells_z, cells_z), 0)
    columns = lax.broadcasted_iota(jnp.int32, (cells_z, cells_z), 1)
    apart = jnp.abs(rows - columns)
    band = jnp.zeros((cells_z, cells_z), jnp.float32)
    for distance in range(1, 5):
        band = jnp.where(apart == distance, stencil[distance], band)
    high, low = split_halves(band)
    return jnp.concatenate([high, high, low], axis=0)


def kernel(
    count,
    velocity,
    source_prior,
    source_now,
    record_prior,
    record_now,
    source_x,
    source_y,
    source_t,
    record_x,
    record_y,
    record_t,
    offsets_row,
    offsets,
    images,
    adjoint_source,
    adjoint_record,
    wide0,
    wide1,
    final,
    padded,
    partial,
    added,
    squares,
    weights,
    send0,
    recv0,
    send1,
    recv1,
    send2,
    recv2,
):
    extent, cells_y, cells_z = velocity.shape
    lags = images.shape[0]
    me = lax.axis_index("gx")
    has_lower = me > 0
    has_upper = me < count - 1
    lower = jnp.maximum(me - 1, 0)
    upper = jnp.minimum(me + 1, count - 1)
    nows = (source_now, record_now)
    priors = (source_prior, record_prior)

    def copy(src, dst, send, recv, device):
        return pltpu.make_async_remote_copy(
            src_ref=src,
            dst_ref=dst,
            send_sem=send,
            recv_sem=recv,
            device_id={"gx": device},
            device_id_type=pl.DeviceIdType.MESH,
        )

    down, up = [], []
    for f in range(2):
        down.append(copy(nows[f].at[pl.ds(0, RIM)], wide0.at[f, pl.ds(RIM + extent, RIM)], send0.at[f], recv0.at[f], lower))
        up.append(copy(nows[f].at[pl.ds(extent - RIM, RIM)], wide0.at[f, pl.ds(0, RIM)], send0.at[2 + f], recv0.at[2 + f], upper))
    first = (down, up)
    second = (
        [copy(wide1.at[:, pl.ds(RIM, RIM)], wide1.at[:, pl.ds(RIM + extent, RIM)], send1.at[0], recv1.at[0], lower)],
        [copy(wide1.at[:, pl.ds(extent, RIM)], wide1.at[:, pl.ds(0, RIM)], send1.at[1], recv1.at[1], upper)],
    )

    def final_copies(start, length, slot):
        src = final.at[:, pl.ds(REACH + start, length)]
        return (
            copy(src, final.at[:, pl.ds(REACH + extent + start, length)], send2.at[slot], recv2.at[slot], lower),
            copy(src, final.at[:, pl.ds(REACH - extent + start, length)], send2.at[3 + slot], recv2.at[3 + slot], upper),
        )

    pieces = ((RIM, extent - 2 * RIM), (0, RIM), (extent - RIM, RIM))
    third = [final_copies(start, length, slot) for slot, (start, length) in enumerate(pieces)]

    def start(group):
        @pl.when(has_lower)
        def _():
            for one in group[0]:
                one.start()

        @pl.when(has_upper)
        def _():
            for one in group[1]:
                one.start()

    def arrive(group):
        @pl.when(has_upper)
        def _():
            for one in group[0]:
                one.wait_recv()

        @pl.when(has_lower)
        def _():
            for one in group[1]:
                one.wait_recv()

    def leave(group):
        @pl.when(has_lower)
        def _():
            for one in group[0]:
                one.wait_send()

        @pl.when(has_upper)
        def _():
            for one in group[1]:
                one.wait_send()

    barrier = pltpu.get_barrier_semaphore()

    @pl.when(has_lower)
    def _():
        pl.semaphore_signal(barrier, inc=1, device_id={"gx": lower}, device_id_type=pl.DeviceIdType.MESH)

    @pl.when(has_upper)
    def _():
        pl.semaphore_signal(barrier, inc=1, device_id={"gx": upper}, device_id_type=pl.DeviceIdType.MESH)

    @pl.when(jnp.logical_not(has_lower))
    def _():
        wide0[:, pl.ds(0, RIM)] = jnp.zeros((2, RIM, cells_y, cells_z), jnp.float32)
        wide1[:, pl.ds(0, RIM)] = jnp.zeros((2, RIM, cells_y, cells_z), jnp.float32)
        final[:, pl.ds(0, REACH)] = jnp.zeros((2, REACH, cells_y, cells_z), jnp.float32)

    @pl.when(jnp.logical_not(has_upper))
    def _():
        wide0[:, pl.ds(RIM + extent, RIM)] = jnp.zeros((2, RIM, cells_y, cells_z), jnp.float32)
        wide1[:, pl.ds(RIM + extent, RIM)] = jnp.zeros((2, RIM, cells_y, cells_z), jnp.float32)
        final[:, pl.ds(REACH + extent, REACH)] = jnp.zeros((2, REACH, cells_y, cells_z), jnp.float32)

    pl.semaphore_wait(barrier, has_lower.astype(jnp.int32) + has_upper.astype(jnp.int32))

    start(first)

    padded[:, :, pl.ds(0, LEFT_PAD)] = jnp.zeros((2, extent, LEFT_PAD, cells_z), jnp.float32)
    padded[:, :, pl.ds(LEFT_PAD + cells_y, LEFT_PAD)] = jnp.zeros((2, extent, LEFT_PAD, cells_z), jnp.float32)
    for f in range(2):
        wide0[f, pl.ds(RIM, extent)] = nows[f][...]
        padded[f, :, pl.ds(LEFT_PAD, cells_y)] = nows[f][...]

    rows = extent * cells_y
    for f, (place_x, place_y, pulse) in enumerate(((source_x, source_y, source_t), (record_x, record_y, record_t))):
        number = place_x.shape[1]
        cell = (place_x[...] - me * extent) * cells_y + place_y[...]
        hits = jnp.where(lax.broadcasted_iota(jnp.int32, (rows, number), 0) == cell, 1.0, 0.0).astype(jnp.bfloat16)
        line = lax.broadcasted_iota(jnp.int32, (STEPS * cells_z, number), 0)
        spread = jnp.zeros((STEPS * cells_z, number), jnp.float32)
        for moment in range(STEPS):
            spread = jnp.where(line == moment * cells_z + depths[f], pulse[pl.ds(moment, 1), :], spread)
        plane = jnp.zeros((rows, STEPS * cells_z), jnp.float32)
        for part in split_halves(spread):
            plane = plane + lax.dot_general(hits, part, (((1,), (1,)), ((), ())), preferred_element_type=jnp.float32)
        for moment in range(STEPS):
            added[moment, f] = plane[:, moment * cells_z : (moment + 1) * cells_z].reshape(extent, cells_y, cells_z)

    band = depth_band(cells_z)

    def beside(moment, wide, before):
        for f in range(2):
            flat = wide[f, pl.ds(RIM, extent)].reshape(rows, cells_z)
            high, low = split_halves(flat)
            along = jnp.dot(jnp.concatenate([high, low, high], axis=1), band, preferred_element_type=jnp.float32)
            along = along.reshape(extent, cells_y, cells_z)
            for x in range(0, extent, RIM):
                centre = wide[f, pl.ds(RIM + x, RIM)]
                total = 3.0 * stencil[0] * centre + along[x : x + RIM]
                for distance in range(1, 5):
                    pair = padded[f, pl.ds(x, RIM), pl.ds(LEFT_PAD - distance, cells_y)] + padded[f, pl.ds(x, RIM), pl.ds(LEFT_PAD + distance, cells_y)]
                    total = total + stencil[distance] * pair
                partial[f, pl.ds(x, RIM)] = (
                    2.0 * centre - before(f, x) + velocity[pl.ds(x, RIM)] * total + added[moment, f, pl.ds(x, RIM)]
                )

    def finished(wide, f, x):
        total = None
        for distance in range(1, 5):
            pair = wide[f, pl.ds(RIM + x - distance, RIM)] + wide[f, pl.ds(RIM + x + distance, RIM)]
            term = stencil[distance] * pair
            total = term if total is None else total + term
        return partial[f, pl.ds(x, RIM)] + velocity[pl.ds(x, RIM)] * total

    inner = range(RIM, extent - RIM, RIM)
    edges = (0, extent - RIM)

    def keep_first(f, x):
        value = finished(wide0, f, x)
        wide1[f, pl.ds(RIM + x, RIM)] = value
        padded[f, pl.ds(x, RIM), pl.ds(LEFT_PAD, cells_y)] = value

    def keep_final(f, x):
        value = finished(wide1, f, x)
        final[f, pl.ds(REACH + x, RIM)] = value
        squares[f, pl.ds(REACH + x, RIM)] = value * value

    beside(0, wide0, lambda f, x: priors[f][pl.ds(x, RIM)])
    for f in range(2):
        for x in inner:
            keep_first(f, x)
    arrive(first)
    for f in range(2):
        for x in edges:
            keep_first(f, x)
    start(second)

    beside(1, wide1, lambda f, x: wide0[f, pl.ds(RIM + x, RIM)])
    for f in range(2):
        for x in inner:
            keep_final(f, x)
    start(([third[0][0]], [third[0][1]]))
    arrive(second)
    for f in range(2):
        for x in edges:
            keep_final(f, x)
    start(([third[1][0], third[2][0]], [third[2][1], third[1][1]]))

    signed = lax.broadcasted_iota(jnp.int32, (2 * LAG_MAX + 1, lags), 0) - LAG_MAX
    same = jnp.where(signed == offsets_row[...], 1.0, 0.0)
    tally = jnp.sum(same, axis=1, keepdims=True)
    signed_column = lax.broadcasted_iota(jnp.int32, (2 * LAG_MAX + 1, cells_z), 0) - LAG_MAX
    weight = (signed_column * signed_column).astype(jnp.float32) / (LAG_MAX * LAG_MAX * lags)
    weights[pl.ds(0, 2 * LAG_MAX + 1), :] = weight * tally

    arrive(([one[0] for one in third], [one[1] for one in third]))

    def picture(k, carry):
        shift = offsets[k]
        left = final[0, pl.ds(REACH - shift, extent)]
        right = final[1, pl.ds(REACH + shift, extent)]
        images[k] = (left * right).astype(jnp.bfloat16)
        return carry

    lax.fori_loop(0, lags, picture, 0)

    for f in range(2):
        for side in (0, REACH + extent):
            value = final[f, pl.ds(side, REACH)]
            squares[f, pl.ds(side, REACH)] = value * value
    for f, out in ((0, adjoint_source), (1, adjoint_record)):
        sign = 2 if f == 0 else -2
        for x in range(0, extent, RIM):
            total = None
            for lag in range(-LAG_MAX, LAG_MAX + 1):
                if lag == 0:
                    continue
                term = weights[pl.ds(lag + LAG_MAX, 1), :] * squares[1 - f, pl.ds(REACH + x + sign * lag, RIM)]
                total = term if total is None else total + term
            out[pl.ds(x, RIM)] = final[f, pl.ds(REACH + x, RIM)] * total

    leave(first)
    leave(second)
    leave(([one[0] for one in third], [one[1] for one in third]))


def per_device(
    velocity,
    source_prior,
    source_now,
    record_prior,
    record_now,
    source_inline,
    source_crossline,
    source_pulse,
    receiver_inline,
    receiver_crossline,
    receiver_trace,
    offsets,
):
    extent, cells_y, cells_z = velocity.shape
    lags = offsets.shape[0]
    field = jax.ShapeDtypeStruct(velocity.shape, jnp.float32)
    vmem = pl.BlockSpec(memory_space=pltpu.VMEM)
    smem = pl.BlockSpec(memory_space=pltpu.SMEM)
    call = pl.pallas_call(
        functools.partial(kernel, lax.axis_size("gx")),
        out_shape=(jax.ShapeDtypeStruct((lags,) + velocity.shape, jnp.bfloat16), field, field),
        in_specs=[vmem] * 12 + [smem],
        out_specs=(vmem, vmem, vmem),
        scratch_shapes=[
            pltpu.VMEM((2, extent + 2 * RIM, cells_y, cells_z), jnp.float32),
            pltpu.VMEM((2, extent + 2 * RIM, cells_y, cells_z), jnp.float32),
            pltpu.VMEM((2, extent + 2 * REACH, cells_y, cells_z), jnp.float32),
            pltpu.VMEM((2, extent, cells_y + 2 * LEFT_PAD, cells_z), jnp.float32),
            pltpu.VMEM((2, extent, cells_y, cells_z), jnp.float32),
            pltpu.VMEM((STEPS, 2, extent, cells_y, cells_z), jnp.float32),
            pltpu.VMEM((2, extent + 2 * REACH, cells_y, cells_z), jnp.float32),
            pltpu.VMEM((2 * LAG_MAX + 8, cells_z), jnp.float32),
            pltpu.SemaphoreType.DMA((4,)),
            pltpu.SemaphoreType.DMA((4,)),
            pltpu.SemaphoreType.DMA((2,)),
            pltpu.SemaphoreType.DMA((2,)),
            pltpu.SemaphoreType.DMA((6,)),
            pltpu.SemaphoreType.DMA((6,)),
        ],
        compiler_params=pltpu.CompilerParams(
            collective_id=0, has_side_effects=True, vmem_limit_bytes=40 * 1024 * 1024
        ),
    )
    return call(
        velocity,
        source_prior,
        source_now,
        record_prior,
        record_now,
        source_inline.reshape(1, -1),
        source_crossline.reshape(1, -1),
        source_pulse.T,
        receiver_inline.reshape(1, -1),
        receiver_crossline.reshape(1, -1),
        receiver_trace.T,
        offsets.reshape(1, -1),
        offsets,
    )


def solution(mesh):
    in_specs = (
        P("gx", None, None),
        P(("shots", "gx"), None, None),
        P(("shots", "gx"), None, None),
        P(("shots", "gx"), None, None),
        P(("shots", "gx"), None, None),
        P("shots"),
        P("shots"),
        P("shots", None),
        P("shots"),
        P("shots"),
        P("shots", None),
        P(),
    )
    out_specs = (
        P("shots", "gx", None, None),
        P(("shots", "gx"), None, None),
        P(("shots", "gx"), None, None),
    )
    return jax.shard_map(
        per_device, mesh=mesh, in_specs=in_specs, out_specs=out_specs, check_vma=False
    )
```

time: 125 us -> 32.4 us (0.26)
  the two profiles are of different devices: /device:TPU:8 before, /device:TPU:9 now
where the time goes in v1:
time: 32.4 us; the launch traced here: 32 us
  Pallas kernels  19.5 us (60%)
  local copies, waits for them, and re-layouts  11.9 us (37%)
  between operations  0.66 us (2%)
    pallas_call x1, Pallas kernels, per_device(): call(velocity, source_prior, source_now, record_prior, record_now, source...  19.5 us
    unnamed x27, local copies, waits for them, and re-layouts  11.9 us

profile of v1, /device:TPU:9, one launch (start us, length us, event | category | flops | bytes accessed | tf_op | source)
XLA Modules:
  0.0 32.0 jit_solution(11211526926582151207)
XLA Ops:
  0.6 0.0 copy-start
  0.6 0.9 %copy-done = f32[16,24,128]{2,1,0:T(8,128)S(1)} copy-done((f32[16,24,128]{2,1,0:T(8,128)S(1)}, f32[16,24,128]{2,1,0:T(8,128)}, u32[]{:S(2)}) %copy-start) | copy-done | bytes 196632
  1.6 0.0 copy-start.1
  1.6 0.9 %copy-done.1 = f32[16,24,128]{2,1,0:T(8,128)S(1)} copy-done((f32[16,24,128]{2,1,0:T(8,128)S(1)}, f32[16,24,128]{2,1,0:T(8,128)}, u32[]{:S(2)}) %copy-start.1) | copy-done | bytes 196632
  2.5 0.0 copy-start.2
  2.5 0.9 %copy-done.2 = f32[16,24,128]{2,1,0:T(8,128)S(1)} copy-done((f32[16,24,128]{2,1,0:T(8,128)S(1)}, f32[16,24,128]{2,1,0:T(8,128)}, u32[]{:S(2)}) %copy-start.2) | copy-done | bytes 196632
  3.4 0.0 copy-start.3
  3.4 0.9 %copy-done.3 = f32[16,24,128]{2,1,0:T(8,128)S(1)} copy-done((f32[16,24,128]{2,1,0:T(8,128)S(1)}, f32[16,24,128]{2,1,0:T(8,128)}, u32[]{:S(2)}) %copy-start.3) | copy-done | bytes 196632
  4.3 0.0 copy-start.4
  4.3 0.9 %copy-done.4 = f32[16,24,128]{2,1,0:T(8,128)S(1)} copy-done((f32[16,24,128]{2,1,0:T(8,128)S(1)}, f32[16,24,128]{2,1,0:T(8,128)}, u32[]{:S(2)}) %copy-start.4) | copy-done | bytes 196632
  5.3 0.0 copy-start.5
  5.3 0.7 %copy-done.5 = f32[1024,2]{0,1:T(2,128)S(1)} copy-done((f32[1024,2]{0,1:T(2,128)S(1)}, f32[1024,2]{0,1:T(2,128)}, u32[]{:S(2)}) %copy-start.5) | copy-done | bytes 8216
  6.0 0.0 copy-start.6
  6.0 0.7 %copy-done.6 = s32[1024]{0:T(1024)S(1)} copy-done((s32[1024]{0:T(1024)S(1)}, s32[1024]{0:T(1024)}, u32[]{:S(2)}) %copy-start.6) | copy-done | bytes 4120
  6.7 0.0 copy-start.7
  6.7 0.7 %copy-done.7 = s32[1024]{0:T(1024)S(1)} copy-done((s32[1024]{0:T(1024)S(1)}, s32[1024]{0:T(1024)}, u32[]{:S(2)}) %copy-start.7) | copy-done | bytes 4120
  7.3 0.0 copy-start.8
  7.3 0.7 %copy-done.8 = s32[17]{0:T(128)S(1)} copy-done((s32[17]{0:T(128)S(1)}, s32[17]{0:T(128)}, u32[]{:S(2)}) %copy-start.8) | copy-done | bytes 92
  8.0 0.0 copy-start.9
  8.0 0.7 %copy-done.9 = f32[16,2]{0,1:T(2,128)S(1)} copy-done((f32[16,2]{0,1:T(2,128)S(1)}, f32[16,2]{0,1:T(2,128)}, u32[]{:S(2)}) %copy-start.9) | copy-done | bytes 152
  8.7 0.0 copy-start.10
  8.7 0.7 %copy-done.10 = s32[16]{0:T(128)S(1)} copy-done((s32[16]{0:T(128)S(1)}, s32[16]{0:T(128)}, u32[]{:S(2)}) %copy-start.10) | copy-done | bytes 88
  9.3 0.0 copy-start.11
  9.3 0.7 %copy-done.11 = s32[16]{0:T(128)S(1)} copy-done((s32[16]{0:T(128)S(1)}, s32[16]{0:T(128)}, u32[]{:S(2)}) %copy-start.11) | copy-done | bytes 88
  10.0 19.5 %shard_map.139 = (bf16[17,16,24,128]{3,2,1,0:T(8,128)(2,1)S(1)}, f32[16,24,128]{2,1,0:T(8,128)S(1)}, f32[16,24,128]{2,1,0:T(8,128)S(1)}) custom-call(f32[16,24,128]{2,1,0:T(8,128)S(1)} %copy-done, f32[16,24,128]{2,1,0:T(8,128)S(1)} %copy-done.1, f32[16,24,128]{2,1,0:T(8,128)S(1)} %copy-done.2, f32[16,24,128]{2,1,0:T(8,128)S(1)} %copy-done.3, ...), custom_call_target="tpu_custom_call" | custom-call | tf_op jit(solution)/shard_map/pallas_call | solution.py:332
  29.5 1.2 %copy.18 = bf16[17,16,24,128]{3,2,1,0:T(8,128)(2,1)} copy(bf16[17,16,24,128]{3,2,1,0:T(8,128)(2,1)S(1)} %get-tuple-element.6) | data formatting | bytes 3342336
  30.7 0.7 %copy.19 = f32[16,24,128]{2,1,0:T(8,128)} copy(f32[16,24,128]{2,1,0:T(8,128)S(1)} %get-tuple-element.7) | data formatting | bytes 393216
  31.3 0.7 %copy.20 = f32[16,24,128]{2,1,0:T(8,128)} copy(f32[16,24,128]{2,1,0:T(8,128)S(1)} %get-tuple-element.8) | data formatting | bytes 393216
Async XLA Ops:
  0.6 0.9 %copy-start = (f32[16,24,128]{2,1,0:T(8,128)S(1)}, f32[16,24,128]{2,1,0:T(8,128)}, u32[]{:S(2)}) copy-start(f32[16,24,128]{2,1,0:T(8,128)} %velocity.1) | copy-start | bytes 589828
  1.6 0.9 %copy-start.1 = (f32[16,24,128]{2,1,0:T(8,128)S(1)}, f32[16,24,128]{2,1,0:T(8,128)}, u32[]{:S(2)}) copy-start(f32[16,24,128]{2,1,0:T(8,128)} %source_prior.1) | copy-start | bytes 589828
  2.5 0.9 %copy-start.2 = (f32[16,24,128]{2,1,0:T(8,128)S(1)}, f32[16,24,128]{2,1,0:T(8,128)}, u32[]{:S(2)}) copy-start(f32[16,24,128]{2,1,0:T(8,128)} %source_now.1) | copy-start | bytes 589828
  3.4 0.9 %copy-start.3 = (f32[16,24,128]{2,1,0:T(8,128)S(1)}, f32[16,24,128]{2,1,0:T(8,128)}, u32[]{:S(2)}) copy-start(f32[16,24,128]{2,1,0:T(8,128)} %record_prior.1) | copy-start | bytes 589828
  4.3 0.9 %copy-start.4 = (f32[16,24,128]{2,1,0:T(8,128)S(1)}, f32[16,24,128]{2,1,0:T(8,128)}, u32[]{:S(2)}) copy-start(f32[16,24,128]{2,1,0:T(8,128)} %record_now.1) | copy-start | bytes 589828
  5.3 0.7 %copy-start.5 = (f32[1024,2]{0,1:T(2,128)S(1)}, f32[1024,2]{0,1:T(2,128)}, u32[]{:S(2)}) copy-start(f32[1024,2]{0,1:T(2,128)} %param.22) | copy-start | bytes 24580
  6.0 0.7 %copy-start.6 = (s32[1024]{0:T(1024)S(1)}, s32[1024]{0:T(1024)}, u32[]{:S(2)}) copy-start(s32[1024]{0:T(1024)} %param.20) | copy-start | bytes 12292
  6.7 0.7 %copy-start.7 = (s32[1024]{0:T(1024)S(1)}, s32[1024]{0:T(1024)}, u32[]{:S(2)}) copy-start(s32[1024]{0:T(1024)} %param.21) | copy-start | bytes 12292
  7.3 0.7 %copy-start.8 = (s32[17]{0:T(128)S(1)}, s32[17]{0:T(128)}, u32[]{:S(2)}) copy-start(s32[17]{0:T(128)} %offsets.1) | copy-start | bytes 208
  8.0 0.7 %copy-start.9 = (f32[16,2]{0,1:T(2,128)S(1)}, f32[16,2]{0,1:T(2,128)}, u32[]{:S(2)}) copy-start(f32[16,2]{0,1:T(2,128)} %param.19) | copy-start | bytes 388
  8.7 0.7 %copy-start.10 = (s32[16]{0:T(128)S(1)}, s32[16]{0:T(128)}, u32[]{:S(2)}) copy-start(s32[16]{0:T(128)} %param.17) | copy-start | bytes 196
  9.3 0.7 %copy-start.11 = (s32[16]{0:T(128)S(1)}, s32[16]{0:T(128)}, u32[]{:S(2)}) copy-start(s32[16]{0:T(128)} %param.18) | copy-start | bytes 196

commit v2 on v1

--- a/solution.py
+++ b/solution.py
@@ -36,19 +36,19 @@
 
 def kernel(
     count,
-    velocity,
+    velocity_hbm,
     source_prior,
     source_now,
     record_prior,
     record_now,
-    source_x,
-    source_y,
-    source_t,
-    record_x,
-    record_y,
-    record_t,
-    offsets_row,
-    offsets,
+    source_x_hbm,
+    source_y_hbm,
+    source_t_hbm,
+    record_x_hbm,
+    record_y_hbm,
+    record_t_hbm,
+    offsets_row_hbm,
+    offsets_hbm,
     images,
     adjoint_source,
     adjoint_record,
@@ -66,9 +66,33 @@
     recv1,
     send2,
     recv2,
+    velocity,
+    prior,
+    source_x,
+    source_y,
+    source_t,
+    record_x,
+    record_y,
+    record_t,
+    offsets_row,
+    offsets,
+    loaded,
 ):
     extent, cells_y, cells_z = velocity.shape
     lags = images.shape[0]
+    small = [
+        pltpu.make_async_copy(src, dst, loaded.at[slot])
+        for slot, (src, dst) in enumerate((
+            (record_x_hbm, record_x),
+            (record_y_hbm, record_y),
+            (record_t_hbm, record_t),
+            (source_x_hbm, source_x),
+            (source_y_hbm, source_y),
+            (source_t_hbm, source_t),
+            (offsets_row_hbm, offsets_row),
+            (offsets_hbm, offsets),
+        ))
+    ]
     me = lax.axis_index("gx")
     has_lower = me > 0
     has_upper = me < count - 1
@@ -140,6 +164,17 @@
             for one in group[1]:
                 one.wait_send()
 
+    large = []
+    for f in range(2):
+        large.append((nows[f], wide0.at[f, pl.ds(RIM, extent)]))
+        large.append((nows[f], padded.at[f, :, pl.ds(LEFT_PAD, cells_y)]))
+        large.append((priors[f], prior.at[f]))
+    large.append((velocity_hbm, velocity))
+    large = [
+        pltpu.make_async_copy(src, dst, loaded.at[len(small) + slot])
+        for slot, (src, dst) in enumerate(large)
+    ]
+
     barrier = pltpu.get_barrier_semaphore()
 
     @pl.when(has_lower)
@@ -149,6 +184,9 @@
     @pl.when(has_upper)
     def _():
         pl.semaphore_signal(barrier, inc=1, device_id={"gx": upper}, device_id_type=pl.DeviceIdType.MESH)
+
+    for one in small + large:
+        one.start()
 
     @pl.when(jnp.logical_not(has_lower))
     def _():
@@ -168,9 +206,8 @@
 
     padded[:, :, pl.ds(0, LEFT_PAD)] = jnp.zeros((2, extent, LEFT_PAD, cells_z), jnp.float32)
     padded[:, :, pl.ds(LEFT_PAD + cells_y, LEFT_PAD)] = jnp.zeros((2, extent, LEFT_PAD, cells_z), jnp.float32)
-    for f in range(2):
-        wide0[f, pl.ds(RIM, extent)] = nows[f][...]
-        padded[f, :, pl.ds(LEFT_PAD, cells_y)] = nows[f][...]
+    for one in small:
+        one.wait()
 
     rows = extent * cells_y
     for f, (place_x, place_y, pulse) in enumerate(((source_x, source_y, source_t), (record_x, record_y, record_t))):
@@ -226,7 +263,9 @@
         final[f, pl.ds(REACH + x, RIM)] = value
         squares[f, pl.ds(REACH + x, RIM)] = value * value
 
-    beside(0, wide0, lambda f, x: priors[f][pl.ds(x, RIM)])
+    for one in large:
+        one.wait()
+    beside(0, wide0, lambda f, x: prior[f, pl.ds(x, RIM)])
     for f in range(2):
         for x in inner:
             keep_first(f, x)
@@ -283,6 +322,15 @@
     leave(first)
     leave(second)
     leave(([one[0] for one in third], [one[1] for one in third]))
+
+
+def write_out(*refs):
+    count = (len(refs) - 1) // 2
+    copies = [pltpu.make_async_copy(refs[i], refs[count + i], refs[-1].at[i]) for i in range(count)]
+    for one in copies:
+        one.start()
+    for one in copies:
+        one.wait()
 
 
 def per_device(
@@ -303,11 +351,13 @@
     lags = offsets.shape[0]
     field = jax.ShapeDtypeStruct(velocity.shape, jnp.float32)
     vmem = pl.BlockSpec(memory_space=pltpu.VMEM)
-    smem = pl.BlockSpec(memory_space=pltpu.SMEM)
+    hbm = pl.BlockSpec(memory_space=pltpu.HBM)
+    shapes = (jax.ShapeDtypeStruct((lags,) + velocity.shape, jnp.bfloat16), field, field)
+    sources, receivers = source_inline.shape[0], receiver_inline.shape[0]
     call = pl.pallas_call(
         functools.partial(kernel, lax.axis_size("gx")),
-        out_shape=(jax.ShapeDtypeStruct((lags,) + velocity.shape, jnp.bfloat16), field, field),
-        in_specs=[vmem] * 12 + [smem],
+        out_shape=shapes,
+        in_specs=[hbm] * 13,
         out_specs=(vmem, vmem, vmem),
         scratch_shapes=[
             pltpu.VMEM((2, extent + 2 * RIM, cells_y, cells_z), jnp.float32),
@@ -324,12 +374,23 @@
             pltpu.SemaphoreType.DMA((2,)),
             pltpu.SemaphoreType.DMA((6,)),
             pltpu.SemaphoreType.DMA((6,)),
+            pltpu.VMEM(velocity.shape, jnp.float32),
+            pltpu.VMEM((2,) + velocity.shape, jnp.float32),
+            pltpu.VMEM((1, sources), jnp.int32),
+            pltpu.VMEM((1, sources), jnp.int32),
+            pltpu.VMEM((STEPS, sources), jnp.float32),
+            pltpu.VMEM((1, receivers), jnp.int32),
+            pltpu.VMEM((1, receivers), jnp.int32),
+            pltpu.VMEM((STEPS, receivers), jnp.float32),
+            pltpu.VMEM((1, lags), jnp.int32),
+            pltpu.SMEM((lags,), jnp.int32),
+            pltpu.SemaphoreType.DMA((15,)),
         ],
         compiler_params=pltpu.CompilerParams(
             collective_id=0, has_side_effects=True, vmem_limit_bytes=40 * 1024 * 1024
         ),
     )
-    return call(
+    operands = (
         velocity,
         source_prior,
         source_now,
@@ -344,6 +405,15 @@
         offsets.reshape(1, -1),
         offsets,
     )
+    held = call(*[pltpu.with_memory_space_constraint(one, pltpu.HBM) for one in operands])
+    return pl.pallas_call(
+        write_out,
+        out_shape=shapes,
+        in_specs=[vmem] * len(shapes),
+        out_specs=(hbm,) * len(shapes),
+        scratch_shapes=[pltpu.SemaphoreType.DMA((len(shapes),))],
+        compiler_params=pltpu.CompilerParams(vmem_limit_bytes=4 * 1024 * 1024),
+    )(*held)
 
 
 def solution(mesh):

time: 32.4 us -> 21.5 us (0.66)
  local copies, waits for them, and re-layouts: 11.9 us -> 0 us
  Pallas kernels: 19.5 us -> 20.6 us
    unnamed x27 -> x0, local copies, waits for them, and re-layouts: 11.9 us -> none
    pallas_call x1 -> x2, Pallas kernels: 19.5 us -> 20.6 us  [the longest x1 19.3 us: per_device(): call(*[pltpu.with_memory_space_constraint(one, pltpu.HBM) for one in oper...]
where the time goes in v2:
time: 21.5 us; the launch traced here: 21.3 us
  Pallas kernels  20.6 us (96%)
  between operations  0.64 us (3%)
    pallas_call x1, Pallas kernels, per_device(): call(*[pltpu.with_memory_space_constraint(one, pltpu.HBM) for one in oper...  19.3 us
    pallas_call x1, Pallas kernels, per_device(): pl.pallas_call(write_out, out_shape=shapes, in_specs=[vmem] * len(shapes)...  1.32 us

profile of v2, /device:TPU:9, one launch (start us, length us, event | category | flops | bytes accessed | tf_op | source)
XLA Modules:
  0.0 21.3 jit_solution(10368154831277111178)
XLA Ops:
  0.6 19.3 %shard_map.139 = (bf16[17,16,24,128]{3,2,1,0:T(8,128)(2,1)S(1)}, f32[16,24,128]{2,1,0:T(8,128)S(1)}, f32[16,24,128]{2,1,0:T(8,128)S(1)}) custom-call(f32[16,24,128]{2,1,0:T(8,128)} %velocity_hbm.1, f32[16,24,128]{2,1,0:T(8,128)} %source_prior.1, f32[16,24,128]{2,1,0:T(8,128)} %source_now.1, f32[16,24,128]{2,1,0:T(8,128)} %record_prior.1, ...), custom_call_target="tpu_custom_call" | custom-call | tf_op jit(solution)/shard_map/pallas_call | solution.py:408
  19.9 1.3 %shard_map.140 = (bf16[17,16,24,128]{3,2,1,0:T(8,128)(2,1)}, f32[16,24,128]{2,1,0:T(8,128)}, f32[16,24,128]{2,1,0:T(8,128)}) custom-call(bf16[17,16,24,128]{3,2,1,0:T(8,128)(2,1)S(1)} %get-tuple-element.6.refs_0_, f32[16,24,128]{2,1,0:T(8,128)S(1)} %get-tuple-element.7.refs_1_, f32[16,24,128]{2,1,0:T(8,128)S(1)} %get-tuple-element.8.refs_2_), custom_call_target="tpu_custom_call" | custom-call | tf_op jit(solution)/shard_map/pallas_call | solution.py:409

commit v3 on v2

--- a/solution.py
+++ b/solution.py
@@ -54,7 +54,9 @@
     adjoint_record,
     wide0,
     wide1,
-    final,
+    near,
+    far_low,
+    far_high,
     padded,
     partial,
     added,
@@ -121,15 +123,28 @@
         [copy(wide1.at[:, pl.ds(extent, RIM)], wide1.at[:, pl.ds(0, RIM)], send1.at[1], recv1.at[1], upper)],
     )
 
-    def final_copies(start, length, slot):
-        src = final.at[:, pl.ds(REACH + start, length)]
+    def final_copies(slot, to_lower, length):
+        shared = send2.at[slot], recv2.at[slot]
+        opposite = extent - to_lower - length
+
+        def target(first_cell, low_side):
+            if low_side:
+                if first_cell >= extent - LAG_MAX:
+                    return near.at[:, pl.ds(first_cell - extent + LAG_MAX, length)]
+                return far_low.at[:, pl.ds(first_cell, length)]
+            if first_cell < LAG_MAX:
+                return near.at[:, pl.ds(LAG_MAX + extent + first_cell, length)]
+            return far_high.at[:, pl.ds(first_cell - LAG_MAX, length)]
+
         return (
-            copy(src, final.at[:, pl.ds(REACH + extent + start, length)], send2.at[slot], recv2.at[slot], lower),
-            copy(src, final.at[:, pl.ds(REACH - extent + start, length)], send2.at[3 + slot], recv2.at[3 + slot], upper),
+            [copy(near.at[:, pl.ds(LAG_MAX + to_lower, length)], target(to_lower, False), *shared, lower)],
+            [copy(near.at[:, pl.ds(LAG_MAX + opposite, length)], target(opposite, True), send2.at[4 + slot], recv2.at[4 + slot], upper)],
         )
 
-    pieces = ((RIM, extent - 2 * RIM), (0, RIM), (extent - RIM, RIM))
-    third = [final_copies(start, length, slot) for slot, (start, length) in enumerate(pieces)]
+    near_early = final_copies(0, RIM, LAG_MAX - RIM)
+    far_early = final_copies(1, LAG_MAX, extent - RIM - LAG_MAX)
+    near_late = final_copies(2, 0, RIM)
+    far_late = final_copies(3, extent - RIM, RIM)
 
     def start(group):
         @pl.when(has_lower)
@@ -192,13 +207,15 @@
     def _():
         wide0[:, pl.ds(0, RIM)] = jnp.zeros((2, RIM, cells_y, cells_z), jnp.float32)
         wide1[:, pl.ds(0, RIM)] = jnp.zeros((2, RIM, cells_y, cells_z), jnp.float32)
-        final[:, pl.ds(0, REACH)] = jnp.zeros((2, REACH, cells_y, cells_z), jnp.float32)
+        near[:, pl.ds(0, LAG_MAX)] = jnp.zeros((2, LAG_MAX, cells_y, cells_z), jnp.float32)
+        far_low[...] = jnp.zeros((2, LAG_MAX, cells_y, cells_z), jnp.float32)
 
     @pl.when(jnp.logical_not(has_upper))
     def _():
         wide0[:, pl.ds(RIM + extent, RIM)] = jnp.zeros((2, RIM, cells_y, cells_z), jnp.float32)
         wide1[:, pl.ds(RIM + extent, RIM)] = jnp.zeros((2, RIM, cells_y, cells_z), jnp.float32)
-        final[:, pl.ds(REACH + extent, REACH)] = jnp.zeros((2, REACH, cells_y, cells_z), jnp.float32)
+        near[:, pl.ds(LAG_MAX + extent, LAG_MAX)] = jnp.zeros((2, LAG_MAX, cells_y, cells_z), jnp.float32)
+        far_high[...] = jnp.zeros((2, LAG_MAX, cells_y, cells_z), jnp.float32)
 
     pl.semaphore_wait(barrier, has_lower.astype(jnp.int32) + has_upper.astype(jnp.int32))
 
@@ -226,15 +243,15 @@
 
     band = depth_band(cells_z)
 
-    def beside(moment, wide, before):
+    def beside(moment, wide, before, begin, end):
         for f in range(2):
-            flat = wide[f, pl.ds(RIM, extent)].reshape(rows, cells_z)
+            flat = wide[f, pl.ds(RIM + begin, end - begin)].reshape((end - begin) * cells_y, cells_z)
             high, low = split_halves(flat)
             along = jnp.dot(jnp.concatenate([high, low, high], axis=1), band, preferred_element_type=jnp.float32)
-            along = along.reshape(extent, cells_y, cells_z)
-            for x in range(0, extent, RIM):
+            along = along.reshape(end - begin, cells_y, cells_z)
+            for x in range(begin, end, RIM):
                 centre = wide[f, pl.ds(RIM + x, RIM)]
-                total = 3.0 * stencil[0] * centre + along[x : x + RIM]
+                total = 3.0 * stencil[0] * centre + along[x - begin : x - begin + RIM]
                 for distance in range(1, 5):
                     pair = padded[f, pl.ds(x, RIM), pl.ds(LEFT_PAD - distance, cells_y)] + padded[f, pl.ds(x, RIM), pl.ds(LEFT_PAD + distance, cells_y)]
                     total = total + stencil[distance] * pair
@@ -260,12 +277,12 @@
 
     def keep_final(f, x):
         value = finished(wide1, f, x)
-        final[f, pl.ds(REACH + x, RIM)] = value
+        near[f, pl.ds(LAG_MAX + x, RIM)] = value
         squares[f, pl.ds(REACH + x, RIM)] = value * value
 
     for one in large:
         one.wait()
-    beside(0, wide0, lambda f, x: prior[f, pl.ds(x, RIM)])
+    beside(0, wide0, lambda f, x: prior[f, pl.ds(x, RIM)], 0, extent)
     for f in range(2):
         for x in inner:
             keep_first(f, x)
@@ -275,16 +292,23 @@
             keep_first(f, x)
     start(second)
 
-    beside(1, wide1, lambda f, x: wide0[f, pl.ds(RIM + x, RIM)])
+    def earlier(f, x):
+        return wide0[f, pl.ds(RIM + x, RIM)]
+
+    beside(1, wide1, earlier, RIM, extent - RIM)
     for f in range(2):
         for x in inner:
             keep_final(f, x)
-    start(([third[0][0]], [third[0][1]]))
+    start(near_early)
+    start(far_early)
+    for x in edges:
+        beside(1, wide1, earlier, x, x + RIM)
     arrive(second)
     for f in range(2):
         for x in edges:
             keep_final(f, x)
-    start(([third[1][0], third[2][0]], [third[2][1], third[1][1]]))
+    start(near_late)
+    start(far_late)
 
     signed = lax.broadcasted_iota(jnp.int32, (2 * LAG_MAX + 1, lags), 0) - LAG_MAX
     same = jnp.where(signed == offsets_row[...], 1.0, 0.0)
@@ -293,40 +317,65 @@
     weight = (signed_column * signed_column).astype(jnp.float32) / (LAG_MAX * LAG_MAX * lags)
     weights[pl.ds(0, 2 * LAG_MAX + 1), :] = weight * tally
 
-    arrive(([one[0] for one in third], [one[1] for one in third]))
+    step = 2
+
+    def gather(inside, first, last):
+        for f, out in ((0, adjoint_source), (1, adjoint_record)):
+            sign = 2 if f == 0 else -2
+            for x in range(0, extent, step):
+                total = None if first else partial[f, pl.ds(x, step)]
+                for lag in range(-LAG_MAX, LAG_MAX + 1):
+                    place = x + sign * lag
+                    if lag == 0 or not inside(place):
+                        continue
+                    term = weights[pl.ds(lag + LAG_MAX, 1), :] * squares[1 - f, pl.ds(REACH + place, step)]
+                    total = term if total is None else total + term
+                if last:
+                    out[pl.ds(x, step)] = near[f, pl.ds(LAG_MAX + x, step)] * total
+                else:
+                    partial[f, pl.ds(x, step)] = total
+
+    gather(lambda place: 0 <= place < extent, True, False)
+
+    arrive(near_early)
+    arrive(near_late)
 
     def picture(k, carry):
         shift = offsets[k]
-        left = final[0, pl.ds(REACH - shift, extent)]
-        right = final[1, pl.ds(REACH + shift, extent)]
+        left = near[0, pl.ds(LAG_MAX - shift, extent)]
+        right = near[1, pl.ds(LAG_MAX + shift, extent)]
         images[k] = (left * right).astype(jnp.bfloat16)
         return carry
 
     lax.fori_loop(0, lags, picture, 0)
 
     for f in range(2):
-        for side in (0, REACH + extent):
-            value = final[f, pl.ds(side, REACH)]
-            squares[f, pl.ds(side, REACH)] = value * value
-    for f, out in ((0, adjoint_source), (1, adjoint_record)):
-        sign = 2 if f == 0 else -2
-        for x in range(0, extent, RIM):
-            total = None
-            for lag in range(-LAG_MAX, LAG_MAX + 1):
-                if lag == 0:
-                    continue
-                term = weights[pl.ds(lag + LAG_MAX, 1), :] * squares[1 - f, pl.ds(REACH + x + sign * lag, RIM)]
-                total = term if total is None else total + term
-            out[pl.ds(x, RIM)] = final[f, pl.ds(REACH + x, RIM)] * total
-
-    leave(first)
-    leave(second)
-    leave(([one[0] for one in third], [one[1] for one in third]))
-
-
-def write_out(*refs):
-    count = (len(refs) - 1) // 2
-    copies = [pltpu.make_async_copy(refs[i], refs[count + i], refs[-1].at[i]) for i in range(count)]
+        for side in (0, LAG_MAX + extent):
+            value = near[f, pl.ds(side, LAG_MAX)]
+            squares[f, pl.ds(REACH - LAG_MAX + side, LAG_MAX)] = value * value
+
+    def close(place):
+        return -LAG_MAX <= place < extent + LAG_MAX
+
+    gather(lambda place: close(place) and not 0 <= place < extent, False, False)
+
+    arrive(far_early)
+    arrive(far_late)
+    for f in range(2):
+        for far, side in ((far_low, 0), (far_high, REACH + extent + LAG_MAX)):
+            value = far[f]
+            squares[f, pl.ds(side, LAG_MAX)] = value * value
+    gather(lambda place: not close(place), False, True)
+
+    for group in (first, second, near_early, far_early, near_late, far_late):
+        leave(group)
+
+
+def write_out(images, source, record, images_out, source_out, record_out, done):
+    lags = images.shape[0]
+    copies = [pltpu.make_async_copy(images.at[k], images_out.at[k], done.at[k]) for k in range(lags)]
+    copies.append(pltpu.make_async_copy(source, source_out, done.at[lags]))
+    copies.append(pltpu.make_async_copy(record, record_out, done.at[lags + 1]))
     for one in copies:
         one.start()
     for one in copies:
@@ -362,7 +411,9 @@
         scratch_shapes=[
             pltpu.VMEM((2, extent + 2 * RIM, cells_y, cells_z), jnp.float32),
             pltpu.VMEM((2, extent + 2 * RIM, cells_y, cells_z), jnp.float32),
-            pltpu.VMEM((2, extent + 2 * REACH, cells_y, cells_z), jnp.float32),
+            pltpu.VMEM((2, extent + 2 * LAG_MAX, cells_y, cells_z), jnp.float32),
+            pltpu.VMEM((2, LAG_MAX, cells_y, cells_z), jnp.float32),
+            pltpu.VMEM((2, LAG_MAX, cells_y, cells_z), jnp.float32),
             pltpu.VMEM((2, extent, cells_y + 2 * LEFT_PAD, cells_z), jnp.float32),
             pltpu.VMEM((2, extent, cells_y, cells_z), jnp.float32),
             pltpu.VMEM((STEPS, 2, extent, cells_y, cells_z), jnp.float32),
@@ -372,8 +423,8 @@
             pltpu.SemaphoreType.DMA((4,)),
             pltpu.SemaphoreType.DMA((2,)),
             pltpu.SemaphoreType.DMA((2,)),
-            pltpu.SemaphoreType.DMA((6,)),
-            pltpu.SemaphoreType.DMA((6,)),
+            pltpu.SemaphoreType.DMA((8,)),
+            pltpu.SemaphoreType.DMA((8,)),
             pltpu.VMEM(velocity.shape, jnp.float32),
             pltpu.VMEM((2,) + velocity.shape, jnp.float32),
             pltpu.VMEM((1, sources), jnp.int32),
@@ -411,7 +462,7 @@
         out_shape=shapes,
         in_specs=[vmem] * len(shapes),
         out_specs=(hbm,) * len(shapes),
-        scratch_shapes=[pltpu.SemaphoreType.DMA((len(shapes),))],
+        scratch_shapes=[pltpu.SemaphoreType.DMA((lags + 2,))],
         compiler_params=pltpu.CompilerParams(vmem_limit_bytes=4 * 1024 * 1024),
     )(*held)
 

time: 21.5 us -> 20.8 us (0.967)
  Pallas kernels: 20.6 us -> 20 us
    pallas_call x1, Pallas kernels: 19.3 us -> 18.5 us  [per_device(): call(*[pltpu.with_memory_space_constraint(one, pltpu.HBM) for one in oper...]
where the time goes in v3:
time: 20.8 us; the launch traced here: 20.6 us
  Pallas kernels  20 us (96%)
  between operations  0.64 us (3%)
    pallas_call x1, Pallas kernels, per_device(): call(*[pltpu.with_memory_space_constraint(one, pltpu.HBM) for one in oper...  18.5 us
    pallas_call x1, Pallas kernels, per_device(): pl.pallas_call(write_out, out_shape=shapes, in_specs=[vmem] * len(shapes)...  1.46 us

profile of v3, /device:TPU:9, one launch (start us, length us, event | category | flops | bytes accessed | tf_op | source)
XLA Modules:
  0.0 20.6 jit_solution(1755858528021927649)
XLA Ops:
  0.6 18.5 %shard_map.139 = (bf16[17,16,24,128]{3,2,1,0:T(8,128)(2,1)S(1)}, f32[16,24,128]{2,1,0:T(8,128)S(1)}, f32[16,24,128]{2,1,0:T(8,128)S(1)}) custom-call(f32[16,24,128]{2,1,0:T(8,128)} %velocity_hbm.1, f32[16,24,128]{2,1,0:T(8,128)} %source_prior.1, f32[16,24,128]{2,1,0:T(8,128)} %source_now.1, f32[16,24,128]{2,1,0:T(8,128)} %record_prior.1, ...), custom_call_target="tpu_custom_call" | custom-call | tf_op jit(solution)/shard_map/pallas_call | solution.py:459
  19.2 1.5 %shard_map.140 = (bf16[17,16,24,128]{3,2,1,0:T(8,128)(2,1)}, f32[16,24,128]{2,1,0:T(8,128)}, f32[16,24,128]{2,1,0:T(8,128)}) custom-call(bf16[17,16,24,128]{3,2,1,0:T(8,128)(2,1)S(1)} %get-tuple-element.6.images, f32[16,24,128]{2,1,0:T(8,128)S(1)} %get-tuple-element.7.source, f32[16,24,128]{2,1,0:T(8,128)S(1)} %get-tuple-element.8.record), custom_call_target="tpu_custom_call" | custom-call | tf_op jit(solution)/shard_map/pallas_call | solution.py:460

commit v4 on v3

--- a/solution.py
+++ b/solution.py
@@ -282,15 +282,20 @@
 
     for one in large:
         one.wait()
-    beside(0, wide0, lambda f, x: prior[f, pl.ds(x, RIM)], 0, extent)
-    for f in range(2):
-        for x in inner:
-            keep_first(f, x)
+    def initial(f, x):
+        return prior[f, pl.ds(x, RIM)]
+
+    for x in edges:
+        beside(0, wide0, initial, x, x + RIM)
     arrive(first)
     for f in range(2):
         for x in edges:
             keep_first(f, x)
     start(second)
+    beside(0, wide0, initial, RIM, extent - RIM)
+    for f in range(2):
+        for x in inner:
+            keep_first(f, x)
 
     def earlier(f, x):
         return wide0[f, pl.ds(RIM + x, RIM)]
@@ -371,11 +376,9 @@
         leave(group)
 
 
-def write_out(images, source, record, images_out, source_out, record_out, done):
-    lags = images.shape[0]
-    copies = [pltpu.make_async_copy(images.at[k], images_out.at[k], done.at[k]) for k in range(lags)]
-    copies.append(pltpu.make_async_copy(source, source_out, done.at[lags]))
-    copies.append(pltpu.make_async_copy(record, record_out, done.at[lags + 1]))
+def write_out(*refs):
+    count = (len(refs) - 1) // 2
+    copies = [pltpu.make_async_copy(refs[i], refs[count + i], refs[-1].at[i]) for i in range(count)]
     for one in copies:
         one.start()
     for one in copies:
@@ -462,7 +465,7 @@
         out_shape=shapes,
         in_specs=[vmem] * len(shapes),
         out_specs=(hbm,) * len(shapes),
-        scratch_shapes=[pltpu.SemaphoreType.DMA((lags + 2,))],
+        scratch_shapes=[pltpu.SemaphoreType.DMA((len(shapes),))],
         compiler_params=pltpu.CompilerParams(vmem_limit_bytes=4 * 1024 * 1024),
     )(*held)
 

time: 20.8 us -> 20.7 us (level)
  no operation moved by 1% of the time
where the time goes in v4:
time: 20.7 us; the launch traced here: 20.5 us
  Pallas kernels  19.9 us (96%)
  between operations  0.64 us (3%)
    pallas_call x1, Pallas kernels, per_device(): call(*[pltpu.with_memory_space_constraint(one, pltpu.HBM) for one in oper...  18.5 us
    pallas_call x1, Pallas kernels, per_device(): pl.pallas_call(write_out, out_shape=shapes, in_specs=[vmem] * len(shapes)...  1.32 us

profile of v4, /device:TPU:9, one launch (start us, length us, event | category | flops | bytes accessed | tf_op | source)
XLA Modules:
  0.0 20.5 jit_solution(17362350011114156360)
XLA Ops:
  0.6 18.5 %shard_map.139 = (bf16[17,16,24,128]{3,2,1,0:T(8,128)(2,1)S(1)}, f32[16,24,128]{2,1,0:T(8,128)S(1)}, f32[16,24,128]{2,1,0:T(8,128)S(1)}) custom-call(f32[16,24,128]{2,1,0:T(8,128)} %velocity_hbm.1, f32[16,24,128]{2,1,0:T(8,128)} %source_prior.1, f32[16,24,128]{2,1,0:T(8,128)} %source_now.1, f32[16,24,128]{2,1,0:T(8,128)} %record_prior.1, ...), custom_call_target="tpu_custom_call" | custom-call | tf_op jit(solution)/shard_map/pallas_call | solution.py:462
  19.2 1.3 %shard_map.140 = (bf16[17,16,24,128]{3,2,1,0:T(8,128)(2,1)}, f32[16,24,128]{2,1,0:T(8,128)}, f32[16,24,128]{2,1,0:T(8,128)}) custom-call(bf16[17,16,24,128]{3,2,1,0:T(8,128)(2,1)S(1)} %get-tuple-element.6.refs_0_, f32[16,24,128]{2,1,0:T(8,128)S(1)} %get-tuple-element.7.refs_1_, f32[16,24,128]{2,1,0:T(8,128)S(1)} %get-tuple-element.8.refs_2_), custom_call_target="tpu_custom_call" | custom-call | tf_op jit(solution)/shard_map/pallas_call | solution.py:463

commit v5 on v4

--- a/solution.py
+++ b/solution.py
@@ -118,10 +118,13 @@
         down.append(copy(nows[f].at[pl.ds(0, RIM)], wide0.at[f, pl.ds(RIM + extent, RIM)], send0.at[f], recv0.at[f], lower))
         up.append(copy(nows[f].at[pl.ds(extent - RIM, RIM)], wide0.at[f, pl.ds(0, RIM)], send0.at[2 + f], recv0.at[2 + f], upper))
     first = (down, up)
-    second = (
-        [copy(wide1.at[:, pl.ds(RIM, RIM)], wide1.at[:, pl.ds(RIM + extent, RIM)], send1.at[0], recv1.at[0], lower)],
-        [copy(wide1.at[:, pl.ds(extent, RIM)], wide1.at[:, pl.ds(0, RIM)], send1.at[1], recv1.at[1], upper)],
-    )
+    second = [
+        (
+            [copy(wide1.at[f, pl.ds(RIM, RIM)], wide1.at[f, pl.ds(RIM + extent, RIM)], send1.at[f], recv1.at[f], lower)],
+            [copy(wide1.at[f, pl.ds(extent, RIM)], wide1.at[f, pl.ds(0, RIM)], send1.at[2 + f], recv1.at[2 + f], upper)],
+        )
+        for f in range(2)
+    ]
 
     def final_copies(slot, to_lower, length):
         shared = send2.at[slot], recv2.at[slot]
@@ -291,7 +294,7 @@
     for f in range(2):
         for x in edges:
             keep_first(f, x)
-    start(second)
+        start(second[f])
     beside(0, wide0, initial, RIM, extent - RIM)
     for f in range(2):
         for x in inner:
@@ -308,8 +311,8 @@
     start(far_early)
     for x in edges:
         beside(1, wide1, earlier, x, x + RIM)
-    arrive(second)
-    for f in range(2):
+    for f in range(2):
+        arrive(second[f])
         for x in edges:
             keep_final(f, x)
     start(near_late)
@@ -364,15 +367,24 @@
 
     gather(lambda place: close(place) and not 0 <= place < extent, False, False)
 
+    def middle(place):
+        return -LAG_MAX - RIM <= place < extent + LAG_MAX + RIM
+
+    def square_far(low, high):
+        for f in range(2):
+            value = far_low[f, pl.ds(low, RIM)]
+            squares[f, pl.ds(low, RIM)] = value * value
+            value = far_high[f, pl.ds(high, RIM)]
+            squares[f, pl.ds(REACH + extent + LAG_MAX + high, RIM)] = value * value
+
     arrive(far_early)
+    square_far(LAG_MAX - RIM, 0)
+    gather(lambda place: middle(place) and not close(place), False, False)
     arrive(far_late)
-    for f in range(2):
-        for far, side in ((far_low, 0), (far_high, REACH + extent + LAG_MAX)):
-            value = far[f]
-            squares[f, pl.ds(side, LAG_MAX)] = value * value
-    gather(lambda place: not close(place), False, True)
-
-    for group in (first, second, near_early, far_early, near_late, far_late):
+    square_far(0, LAG_MAX - RIM)
+    gather(lambda place: not middle(place), False, True)
+
+    for group in (first, *second, near_early, far_early, near_late, far_late):
         leave(group)
 
 
@@ -424,8 +436,8 @@
             pltpu.VMEM((2 * LAG_MAX + 8, cells_z), jnp.float32),
             pltpu.SemaphoreType.DMA((4,)),
             pltpu.SemaphoreType.DMA((4,)),
-            pltpu.SemaphoreType.DMA((2,)),
-            pltpu.SemaphoreType.DMA((2,)),
+            pltpu.SemaphoreType.DMA((4,)),
+            pltpu.SemaphoreType.DMA((4,)),
             pltpu.SemaphoreType.DMA((8,)),
             pltpu.SemaphoreType.DMA((8,)),
             pltpu.VMEM(velocity.shape, jnp.float32),

time: 20.7 us -> 20.6 us (level)
  no operation moved by 1% of the time
where the time goes in v5:
time: 20.6 us; the launch traced here: 20.4 us
  Pallas kernels  19.8 us (96%)
  between operations  0.64 us (3%)
    pallas_call x1, Pallas kernels, per_device(): call(*[pltpu.with_memory_space_constraint(one, pltpu.HBM) for one in oper...  18.5 us
    pallas_call x1, Pallas kernels, per_device(): pl.pallas_call(write_out, out_shape=shapes, in_specs=[vmem] * len(shapes)...  1.32 us

profile of v5, /device:TPU:9, one launch (start us, length us, event | category | flops | bytes accessed | tf_op | source)
XLA Modules:
  0.0 20.4 jit_solution(7522494834869573794)
XLA Ops:
  0.6 18.5 %shard_map.139 = (bf16[17,16,24,128]{3,2,1,0:T(8,128)(2,1)S(1)}, f32[16,24,128]{2,1,0:T(8,128)S(1)}, f32[16,24,128]{2,1,0:T(8,128)S(1)}) custom-call(f32[16,24,128]{2,1,0:T(8,128)} %velocity_hbm.1, f32[16,24,128]{2,1,0:T(8,128)} %source_prior.1, f32[16,24,128]{2,1,0:T(8,128)} %source_now.1, f32[16,24,128]{2,1,0:T(8,128)} %record_prior.1, ...), custom_call_target="tpu_custom_call" | custom-call | tf_op jit(solution)/shard_map/pallas_call | solution.py:474
  19.1 1.3 %shard_map.140 = (bf16[17,16,24,128]{3,2,1,0:T(8,128)(2,1)}, f32[16,24,128]{2,1,0:T(8,128)}, f32[16,24,128]{2,1,0:T(8,128)}) custom-call(bf16[17,16,24,128]{3,2,1,0:T(8,128)(2,1)S(1)} %get-tuple-element.6.refs_0_, f32[16,24,128]{2,1,0:T(8,128)S(1)} %get-tuple-element.7.refs_1_, f32[16,24,128]{2,1,0:T(8,128)S(1)} %get-tuple-element.8.refs_2_), custom_call_target="tpu_custom_call" | custom-call | tf_op jit(solution)/shard_map/pallas_call | solution.py:475
